TPU v7x, 512 devices: a whole 4x8x8 slice. The times are simulated.
512 devices in a mesh: dp: 8 (over z), space: 64 (over x, y, core).
Axes of the slice: x: 4, y: 8, z: 8, core: 2. Of those that a mesh axis runs over, the one named last changes fastest.
Arguments:
- fields: bfloat16 [8, 16, 512, 8, 512], P('dp', None, 'space'), may hold values from -6 to 6
- cotangent: bfloat16 [8, 16, 512, 8, 512], P('dp', None, 'space'), may hold values from -6 to 6
- mode_weight: float32 [16, 16, 64, 64], P(None, None, None, 'space'), may hold values from -1.5 to 1.5
- point_weight: float32 [16, 16], replicated, may hold values from -1.5 to 1.5
- bias_vector: float32 [16], replicated, may hold values from -3 to 3
Outputs:
- grad_fields: bfloat16 [8, 16, 512, 8, 512], P('dp', None, 'space')
- grad_mode: float32 [16, 16, 64, 64], P(None, None, None, 'space')
- grad_point: float32 [16, 16], replicated
- grad_bias: float32 [16], replicated
All inputs are finite; a program needn't handle non-finite values.
Results may differ from a plain program's by a relative error of at most 0.015.
Values may be sent and summed in bfloat16 or wider, within the bound.
A program may use at most 64 MiB of HBM per device.

v0:
```python
import functools
import math

import jax
import jax.numpy as jnp
import ml_dtypes
import numpy as np
from jax import lax
from jax.experimental import pallas as pl
from jax.experimental.pallas import tpu as pltpu
from jax.sharding import PartitionSpec as P

MESH = pl.DeviceIdType.MESH
F32 = jnp.float32
BF16 = jnp.bfloat16


def basis_table(number, points):
    half = number // 2
    index = np.arange(number)
    freq = np.where(index < half, index, index - half + 1)
    angle = 2.0 * math.pi * ((freq[:, None] * np.arange(points)[None, :]) % points) / points
    values = np.where((index < half)[:, None], np.cos(angle), np.sin(angle))
    values = values * math.sqrt(2.0 / points)
    values[0] = math.sqrt(1.0 / points)
    return values.astype(np.float32).astype(ml_dtypes.bfloat16)


ERF_STEP = 0.3275911 / math.sqrt(2.0)
ERF_TERMS = [
    0.5 * a for a in (0.254829592, -0.284496736, 1.421413741, -1.453152027, 1.061405429)
]


def gelu_slope(value):
    size = jnp.abs(value)
    below = 1.0 + ERF_STEP * size
    guess = pl.reciprocal(below, approx=True)
    step = guess * (2.0 - below * guess)
    tail = jnp.full_like(value, ERF_TERMS[4])
    for term in ERF_TERMS[3::-1]:
        tail = tail * step + term
    tail = tail * step
    bell = jnp.exp2(value * value * (-0.5 * math.log2(math.e)))
    rest = bell * (size * (1.0 / math.sqrt(2.0 * math.pi)) - tail)
    return jnp.where(value >= 0.0, 1.0 + rest, -rest)


def dot(a, b, ca, cb, precision=None):
    return lax.dot_general(
        a, b, (((ca,), (cb,)), ((), ())), precision=precision, preferred_element_type=F32
    )


def split(value):
    high = value.astype(BF16)
    low = (value - high.astype(F32)).astype(BF16)
    return high, low


def kernel(
    sizes, fields, cot, weight, point, bias, tz, tx, txt,
    out, gm_out, gp_out, gb_out,
    f_v, c_v, g_v, acc_v, out_v, stage, w2, su_v,
    su_s, su_r, mx_s, mx_r, sg_s, sg_r, ad_s, ad_r,
    gm_s, gm_r, gm_a, pt_r,
    f_sem, c_sem, o_sem, s_sem, r_sem, gs_sem, gr_sem, ps_sem, pr_sem,
):
    S, D, Y, C, XO, YW, Z, J = sizes
    A = S // Y
    CY = C * YW
    H = C // 2
    me = lax.axis_index("space")
    dp = lax.axis_index("dp")

    def f_copy(x):
        return pltpu.make_async_copy(fields.at[0, :, x], f_v.at[x], f_sem.at[x])

    def c_copy(x):
        return pltpu.make_async_copy(cot.at[0, :, x], c_v.at[x], c_sem.at[x])

    def o_copy(x):
        return pltpu.make_async_copy(out_v.at[x], out.at[0, :, x], o_sem.at[x])

    for x in range(XO):
        f_copy(x).start()
    for x in range(XO):
        c_copy(x).start()

    barrier = pltpu.get_barrier_semaphore()

    @pl.loop(1, S)
    def _(i):
        pl.semaphore_signal(
            barrier, inc=1, device_id={"space": lax.rem(me + i, S)}, device_id_type=MESH
        )

    @pl.loop(1, D)
    def _(i):
        pl.semaphore_signal(
            barrier, inc=1, device_id={"dp": lax.rem(dp + i, D)}, device_id_type=MESH
        )

    def send_copy(n, src, dst, to):
        return pltpu.make_async_remote_copy(
            src_ref=src, dst_ref=dst, send_sem=s_sem.at[n], recv_sem=r_sem.at[n],
            device_id={"space": to}, device_id_type=MESH,
        )

    def scatter(n, sent, got):
        @pl.loop(1, S)
        def _(i):
            to = lax.rem(me + i, S)
            send_copy(n, sent.at[to], got.at[me], to).start()

        got[pl.ds(me, 1)] = sent[pl.ds(me, 1)]

    def all_of(n, ref):
        some = ref.at[pl.ds(0, S - 1)]
        return send_copy(n, some, some, lax.rem(me + 1, S))

    def rows_of(ref, x):
        return ref[x].reshape(CY, Z)

    @pl.loop(0, XO)
    def _(x):
        f_copy(x).wait()
        stage[pl.ds(x, S, stride=XO), :] = dot(tz[...], rows_of(f_v, x), 1, 1)

    su_s[...] = stage[...].reshape(S, XO, CY).astype(BF16)
    pl.semaphore_wait(barrier, S + D - 2)
    scatter(0, su_s, su_r)

    for c in range(C):
        w2[c] = jnp.concatenate([weight[c, :H, :], weight[c, H:, :]], axis=-1)
    spread = (
        lax.broadcasted_iota(jnp.int32, (CY, C), 0) // YW
        == lax.broadcasted_iota(jnp.int32, (CY, C), 1)
    )
    spread_f = spread.astype(F32)
    spread_b = spread.astype(BF16)
    same = (
        lax.broadcasted_iota(jnp.int32, (CY, CY), 0) % YW
        == lax.broadcasted_iota(jnp.int32, (CY, CY), 1) % YW
    )

    def kron(part, flip):
        rows = dot(spread_b, part, 1, 0 if not flip else 1).astype(BF16)
        return jnp.where(same, dot(rows, spread_b, 1, 1), 0.0).astype(BF16)

    p_high, p_low = split(point[...])
    into_out = jnp.concatenate([kron(p_high, True), kron(p_low, True)], axis=1)
    into_in = jnp.concatenate([kron(p_high, False), kron(p_low, False)], axis=1)
    bias_col = jnp.sum(spread_f * bias[...], axis=1, keepdims=True)

    @pl.loop(0, XO)
    def _(x):
        rows = rows_of(f_v, x)
        acc_v[x] = dot(into_out, jnp.concatenate([rows, rows], axis=0), 1, 0) + bias_col

    lane = lax.broadcasted_iota(jnp.int32, (H, YW, 2 * J), 2)

    def spectrum(got):
        rows = got[...].reshape(S * XO, CY)
        return dot(tx[...], rows, 1, 0).T.reshape(C, YW, 2 * J)

    def back(values, sent):
        high, low = split(values)
        rows = dot(txt[...], jnp.concatenate([high, low], axis=1), 1, 1)
        sent[...] = rows.reshape(S, XO, CY).astype(BF16)

    all_of(0, su_r).wait_recv()
    su_v[...] = spectrum(su_r)
    mixed = []
    for o in range(H):
        total = w2[0, o : o + 1, :] * su_v[0]
        for c in range(1, C):
            total = total + w2[c, o : o + 1, :] * su_v[c]
        mixed.append(total[None])
    mixed = jnp.concatenate(mixed, axis=0)
    mixed = jnp.concatenate(
        [jnp.where(lane < J, mixed, 0.0), jnp.where(lane >= J, mixed, 0.0)], axis=0
    )
    back(mixed.reshape(CY, 2 * J), mx_s)
    scatter(1, mx_s, mx_r)

    all_of(1, mx_r).wait_recv()
    stage[...] = mx_r[...].astype(F32).reshape(S * XO, CY)
    for x in range(XO):
        c_copy(x).wait()

    def slope_step(x, bias_sum):
        modes = stage[pl.ds(x, S, stride=XO), :].T.astype(BF16)
        pre = acc_v[x] + dot(modes, tz[...], 1, 0)
        grad = (rows_of(c_v, x).astype(F32) * gelu_slope(pre)).astype(BF16)
        g_v[x] = grad
        depth = dot(tz[...], grad, 1, 1)
        stage[pl.ds(x, S, stride=XO), :] = depth
        return bias_sum + depth[0:1, :]

    bias_sum = lax.fori_loop(0, XO, slope_step, jnp.zeros((1, CY), F32))
    sg_s[...] = stage[...].reshape(S, XO, CY).astype(BF16)
    scatter(2, sg_s, sg_r)

    def point_step(x, total):
        rows = g_v[x]
        acc_v[x] = dot(into_in, jnp.concatenate([rows, rows], axis=0), 1, 0)
        return total + dot(rows_of(f_v, x), rows, 1, 1)

    pairs = lax.fori_loop(0, XO, point_step, jnp.zeros((CY, CY), F32))
    pairs = jnp.sum(jnp.where(same, pairs, 0.0).reshape(C, YW, CY), axis=1)
    constant = float(np.float32(ml_dtypes.bfloat16(math.sqrt(1.0 / Z))))
    terms = jnp.concatenate(
        [pairs[:H], pairs[H:], jnp.broadcast_to(bias_sum * (1.0 / constant), (H, CY))], axis=1
    )
    source = lax.broadcasted_iota(jnp.int32, (3 * CY, 128), 0)
    fold = (source // CY) * C + (source % CY) // YW == lax.broadcasted_iota(
        jnp.int32, (3 * CY, 128), 1
    )
    tile = dot(terms, fold.astype(F32), 1, 0, precision=lax.Precision.HIGHEST)

    mine_y = lax.rem(me // 2, Y)
    mine_a = (me // (2 * Y)) * 2 + lax.rem(me, 2)

    def to_a(a):
        return {"space": ((a // 2) * Y + mine_y) * 2 + lax.rem(a, 2)}

    def to_y(y):
        return {"space": ((me // (2 * Y)) * Y + y) * 2 + lax.rem(me, 2)}

    def to_dp(d):
        return {"dp": d}

    rounds = [(0, A, mine_a, to_a, 0), (1, Y, mine_y, to_y, A), (2, D, dp, to_dp, A + Y)]

    def p_copy(n, first, last, place):
        return pltpu.make_async_remote_copy(
            src_ref=first, dst_ref=last, send_sem=ps_sem.at[n], recv_sem=pr_sem.at[n],
            device_id=place, device_id_type=MESH,
        )

    def p_send(n, value):
        _, count, mine, place, base = rounds[n]
        pt_r[pl.ds(base + mine, 1)] = value[None]

        @pl.loop(1, count)
        def _(i):
            slot = pt_r.at[base + mine]
            p_copy(n, slot, slot, place(lax.rem(mine + i, count))).start()

    def p_all(n):
        _, count, mine, place, base = rounds[n]
        some = pt_r.at[pl.ds(base, count - 1)]
        return p_copy(n, some, some, place(lax.rem(mine + 1, count)))

    def p_sum(n):
        _, count, _, _, base = rounds[n]
        p_all(n).wait_recv()
        total = pt_r[base]
        for i in range(1, count):
            total = total + pt_r[base + i]
        return total

    p_send(0, tile)

    all_of(2, sg_r).wait_recv()
    spec = spectrum(sg_r)
    pair = jnp.where(lane < J, spec[:H], spec[H:])
    adjoint = []
    for c in range(C):
        total = w2[c, 0:1, :] * pair[0]
        for o in range(1, H):
            total = total + w2[c, o : o + 1, :] * pair[o]
        adjoint.append(total[None])
    back(jnp.concatenate(adjoint, axis=0).reshape(CY, 2 * J), ad_s)
    scatter(3, ad_s, ad_r)

    part = C // D
    for c in range(C):
        gm_s[c // part, c % part] = jnp.sum(su_v[c][None] * pair, axis=1)

    def g_copy(n, first, last, to):
        return pltpu.make_async_remote_copy(
            src_ref=first, dst_ref=last, send_sem=gs_sem.at[n], recv_sem=gr_sem.at[n],
            device_id={"dp": to}, device_id_type=MESH,
        )

    def g_all(n, ref):
        some = ref.at[pl.ds(0, D - 1)]
        return g_copy(n, some, some, lax.rem(dp + 1, D))

    @pl.loop(1, D)
    def _(i):
        to = lax.rem(dp + i, D)
        g_copy(0, gm_s.at[to], gm_r.at[dp], to).start()

    gm_r[pl.ds(dp, 1)] = gm_s[pl.ds(dp, 1)]
    p_send(1, p_sum(0))
    g_all(0, gm_r).wait_recv()
    total = gm_r[0]
    for i in range(1, D):
        total = total + gm_r[i]
    gm_a[pl.ds(dp, 1)] = (total * (1.0 / math.sqrt(D * YW)))[None]

    @pl.loop(1, D)
    def _(i):
        slot = gm_a.at[dp]
        g_copy(1, slot, slot, lax.rem(dp + i, D)).start()

    p_send(2, p_sum(1))

    all_of(3, ad_r).wait_recv()
    stage[...] = ad_r[...].astype(F32).reshape(S * XO, CY)

    @pl.loop(0, XO)
    def _(x):
        modes = stage[pl.ds(x, S, stride=XO), :].T.astype(BF16)
        grad = acc_v[x] + dot(modes, tz[...], 1, 0)
        out_v[x] = grad.astype(BF16).reshape(C, YW, Z)
        o_copy(x).start()

    final = p_sum(2) * (1.0 / math.sqrt(D * S * XO * YW * Z))
    gp_out[...] = jnp.concatenate([final[:, :C], final[:, C : 2 * C]], axis=0)
    gb_out[...] = final[0:1, 2 * C : 3 * C]
    g_all(1, gm_a).wait_recv()
    for c in range(C):
        value = gm_a[c // part, c % part]
        gm_out[c, :H, :] = value[:, :J]
        gm_out[c, H:, :] = value[:, J:]

    all_of(0, su_s).wait_send()
    all_of(1, mx_s).wait_send()
    all_of(2, sg_s).wait_send()
    all_of(3, ad_s).wait_send()
    for n in range(3):
        p_all(n).wait_send()
    g_all(0, gm_s).wait_send()
    g_all(1, gm_a).wait_send()
    for x in range(XO):
        o_copy(x).wait()


def shards(S, D, fields, cotangent, mode_weight, point_weight, bias_vector):
    _, C, XO, YW, Z = fields.shape
    J = mode_weight.shape[2]
    CY = C * YW
    Y = 8 if S == 64 else 2
    A = S // Y
    H = C // 2
    tz = basis_table(S, Z)
    tx = basis_table(J, S * XO)
    tx = np.concatenate([tx, tx], axis=0)
    txt = np.ascontiguousarray(np.concatenate([tx, tx], axis=0).T)
    block = (S, XO, CY)
    vmem = pl.BlockSpec(memory_space=pltpu.VMEM)
    hbm = pl.BlockSpec(memory_space=pl.ANY)
    dma = pltpu.SemaphoreType.DMA
    grad_fields, grad_mode, grad_point, grad_bias = pl.pallas_call(
        functools.partial(kernel, (S, D, Y, C, XO, YW, Z, J)),
        out_shape=(
            jax.ShapeDtypeStruct(fields.shape, BF16),
            jax.ShapeDtypeStruct((C, C, J), F32),
            jax.ShapeDtypeStruct((C, C), F32),
            jax.ShapeDtypeStruct((1, C), F32),
        ),
        in_specs=[hbm, hbm, vmem, vmem, vmem, vmem, vmem, vmem],
        out_specs=(hbm, vmem, vmem, vmem),
        scratch_shapes=[
            pltpu.VMEM((XO, C, YW, Z), BF16),
            pltpu.VMEM((XO, C, YW, Z), BF16),
            pltpu.VMEM((XO, CY, Z), BF16),
            pltpu.VMEM((XO, CY, Z), F32),
            pltpu.VMEM((XO, C, YW, Z), BF16),
            pltpu.VMEM((S * XO, CY), F32),
            pltpu.VMEM((C, H, 2 * J), F32),
            pltpu.VMEM((C, YW, 2 * J), F32),
        ]
        + [pltpu.VMEM(block, BF16)] * 8
        + [
            pltpu.VMEM((D, C // D, H, 2 * J), F32),
            pltpu.VMEM((D, C // D, H, 2 * J), F32),
            pltpu.VMEM((D, C // D, H, 2 * J), F32),
            pltpu.VMEM((A + Y + D, 8, 128), F32),
            dma((XO,)),
            dma((XO,)),
            dma((XO,)),
            dma((4,)),
            dma((4,)),
            dma((2,)),
            dma((2,)),
            dma((3,)),
            dma((3,)),
        ],
        compiler_params=pltpu.CompilerParams(
            collective_id=0, has_side_effects=True, vmem_limit_bytes=32 * 1024 * 1024
        ),
    )(
        fields,
        cotangent,
        mode_weight.reshape(C, C, J),
        point_weight,
        bias_vector.reshape(1, C),
        tz,
        tx,
        txt,
    )
    return (
        grad_fields,
        grad_mode.reshape(mode_weight.shape),
        grad_point,
        grad_bias.reshape(C),
    )


def solution(mesh):
    return jax.shard_map(
        functools.partial(shards, mesh.shape["space"], mesh.shape["dp"]),
        mesh=mesh,
        in_specs=(
            P("dp", None, "space", None, None),
            P("dp", None, "space", None, None),
            P(None, None, None, "space"),
            P(),
            P(),
        ),
        out_specs=(P("dp", None, "space", None, None), P(None, None, None, "space"), P(), P()),
        check_vma=False,
    )
```

profile of v0, /device:TPU:1, one launch (start us, length us, event | category | flops | bytes accessed | tf_op | source)
XLA Modules:
  0.0 66.1 jit_solution(14020755729735814301)
XLA Ops:
  0.6 0.0 copy-start.7
  0.6 0.6 copy-done.7
  1.3 0.0 copy-start
  1.3 1.2 %copy-done = bf16[1,16,8,8,512]{4,3,2,1,0:T(8,128)(2,1)S(1)} copy-done((bf16[1,16,8,8,512]{4,3,2,1,0:T(8,128)(2,1)S(1)}, bf16[1,16,8,8,512]{4,3,2,1,0:T(8,128)(2,1)}, u32[]{:S(2)}) %copy-start) | copy-done | bytes 1048600
  2.5 0.0 copy-start.1
  2.5 1.2 %copy-done.1 = bf16[1,16,8,8,512]{4,3,2,1,0:T(8,128)(2,1)S(1)} copy-done((bf16[1,16,8,8,512]{4,3,2,1,0:T(8,128)(2,1)S(1)}, bf16[1,16,8,8,512]{4,3,2,1,0:T(8,128)(2,1)}, u32[]{:S(2)}) %copy-start.1) | copy-done | bytes 1048600
  3.7 0.0 copy-start.2
  3.7 0.9 %copy-done.2 = bf16[512,256]{1,0:T(8,128)(2,1)S(1)} copy-done((bf16[512,256]{1,0:T(8,128)(2,1)S(1)}, bf16[512,256]{1,0:T(8,128)(2,1)}, u32[]{:S(2)}) %copy-start.2) | copy-done | bytes 262168
  4.7 0.0 copy-start.3
  4.7 0.9 %copy-done.3 = f32[16,16,64,1]{2,3,1,0:T(1,128)S(1)} copy-done((f32[16,16,64,1]{2,3,1,0:T(1,128)S(1)}, f32[16,16,64,1]{2,3,1,0:T(1,128)}, u32[]{:S(2)}) %copy-start.3) | copy-done | bytes 65560
  5.6 0.0 copy-start.4
  5.6 0.9 %copy-done.4 = bf16[128,512]{1,0:T(8,128)(2,1)S(1)} copy-done((bf16[128,512]{1,0:T(8,128)(2,1)S(1)}, bf16[128,512]{1,0:T(8,128)(2,1)}, u32[]{:S(2)}) %copy-start.4) | copy-done | bytes 131096
  6.5 0.0 copy-start.5
  6.5 0.8 %copy-done.5 = bf16[64,512]{1,0:T(8,128)(2,1)S(1)} copy-done((bf16[64,512]{1,0:T(8,128)(2,1)S(1)}, bf16[64,512]{1,0:T(8,128)(2,1)}, u32[]{:S(2)}) %copy-start.5) | copy-done | bytes 65560
  7.3 0.0 copy-start.6
  7.3 0.7 %copy-done.6 = f32[16,16]{1,0:T(8,128)S(1)} copy-done((f32[16,16]{1,0:T(8,128)S(1)}, f32[16,16]{1,0:T(8,128)}, u32[]{:S(2)}) %copy-start.6) | copy-done | bytes 1048
  8.0 55.4 %shard_map.111 = (bf16[1,16,8,8,512]{4,3,2,1,0:T(8,128)(2,1)S(1)}, f32[16,16,64]{2,1,0:T(8,128)S(1)}, f32[16,16]{1,0:T(8,128)S(1)}, f32[1,16]{1,0:T(1,128)S(1)}) custom-call(bf16[1,16,8,8,512]{4,3,2,1,0:T(8,128)(2,1)S(1)} %copy-done, bf16[1,16,8,8,512]{4,3,2,1,0:T(8,128)(2,1)S(1)} %copy-done.1, f32[16,16,64]{2,1,0:T(8,128)S(1)} %bitcast.6, ...), custom_call_target="tpu_custom_call" | custom-call | tf_op jit(solution)/shard_map/pallas_call | solution.py:358
  63.4 1.0 %copy.17 = bf16[1,16,8,8,512]{4,3,2,1,0:T(8,128)(2,1)} copy(bf16[1,16,8,8,512]{4,3,2,1,0:T(8,128)(2,1)S(1)} %get-tuple-element.20) | data formatting | bytes 2097152
  64.4 0.7 copy.18
  65.0 0.6 copy.19
  65.6 0.5 copy.20
Async XLA Ops:
  0.6 0.7 copy-start.7
  1.3 1.2 %copy-start = (bf16[1,16,8,8,512]{4,3,2,1,0:T(8,128)(2,1)S(1)}, bf16[1,16,8,8,512]{4,3,2,1,0:T(8,128)(2,1)}, u32[]{:S(2)}) copy-start(bf16[1,16,8,8,512]{4,3,2,1,0:T(8,128)(2,1)} %fields.1) | copy-start | bytes 3145732
  2.5 1.2 %copy-start.1 = (bf16[1,16,8,8,512]{4,3,2,1,0:T(8,128)(2,1)S(1)}, bf16[1,16,8,8,512]{4,3,2,1,0:T(8,128)(2,1)}, u32[]{:S(2)}) copy-start(bf16[1,16,8,8,512]{4,3,2,1,0:T(8,128)(2,1)} %cot.1) | copy-start | bytes 3145732
  3.7 0.9 %copy-start.2 = (bf16[512,256]{1,0:T(8,128)(2,1)S(1)}, bf16[512,256]{1,0:T(8,128)(2,1)}, u32[]{:S(2)}) copy-start(bf16[512,256]{1,0:T(8,128)(2,1)} %constant.8.clone.txt) | copy-start | bytes 786436
  4.7 0.9 %copy-start.3 = (f32[16,16,64,1]{2,3,1,0:T(1,128)S(1)}, f32[16,16,64,1]{2,3,1,0:T(1,128)}, u32[]{:S(2)}) copy-start(f32[16,16,64,1]{2,3,1,0:T(1,128)} %param.10) | copy-start | bytes 196612
  5.6 0.9 %copy-start.4 = (bf16[128,512]{1,0:T(8,128)(2,1)S(1)}, bf16[128,512]{1,0:T(8,128)(2,1)}, u32[]{:S(2)}) copy-start(bf16[128,512]{1,0:T(8,128)(2,1)} %constant.7.clone.tx) | copy-start | bytes 393220
  6.5 0.8 %copy-start.5 = (bf16[64,512]{1,0:T(8,128)(2,1)S(1)}, bf16[64,512]{1,0:T(8,128)(2,1)}, u32[]{:S(2)}) copy-start(bf16[64,512]{1,0:T(8,128)(2,1)} %constant.6.clone.tz) | copy-start | bytes 196612
  7.3 0.7 %copy-start.6 = (f32[16,16]{1,0:T(8,128)S(1)}, f32[16,16]{1,0:T(8,128)}, u32[]{:S(2)}) copy-start(f32[16,16]{1,0:T(8,128)} %point.1) | copy-start | bytes 3076
where the time goes:
time: 67 us; the launch traced here: 66.1 us
  Pallas kernels  55.4 us (83%)
  local copies, waits for them, and re-layouts  10.1 us (15%)
    pallas_call x1, Pallas kernels, shards(): pl.pallas_call(functools.partial(kernel, (S, D, Y, C, XO, YW, Z, J)), out...  55.4 us
    unnamed x20, local copies, waits for them, and re-layouts  10.1 us

commit v1 on v0

v1 whole, which is shorter than its diff:
```python
import functools
import math

import jax
import jax.numpy as jnp
import ml_dtypes
import numpy as np
from jax import lax
from jax.experimental import pallas as pl
from jax.experimental.pallas import tpu as pltpu
from jax.sharding import PartitionSpec as P

MESH = pl.DeviceIdType.MESH
F32 = jnp.float32
BF16 = jnp.bfloat16


def basis_table(number, points):
    half = number // 2
    index = np.arange(number)
    freq = np.where(index < half, index, index - half + 1)
    angle = 2.0 * math.pi * ((freq[:, None] * np.arange(points)[None, :]) % points) / points
    values = np.where((index < half)[:, None], np.cos(angle), np.sin(angle))
    values = values * math.sqrt(2.0 / points)
    values[0] = math.sqrt(1.0 / points)
    return values.astype(np.float32).astype(ml_dtypes.bfloat16)


def gelu_slope(value):
    scaled = value * math.sqrt(0.5)
    bell = jnp.exp2(scaled * scaled * (-math.log2(math.e)))
    return 0.5 + 0.5 * lax.erf(scaled) + scaled * (bell * (1.0 / math.sqrt(math.pi)))


def dot(a, b, ca, cb, precision=None):
    return lax.dot_general(
        a, b, (((ca,), (cb,)), ((), ())), precision=precision, preferred_element_type=F32
    )


def split(value):
    high = value.astype(BF16)
    low = (value - high.astype(F32)).astype(BF16)
    return high, low


def layer_kernel(
    sizes, fields, cot, weight_in, point_in, bias_in, tz_in, tx_in, txt_in,
    acc_v, ad_out, su_out, sg_out, sum_out, tz,
    f_v, c_v, g_v, stage, w2, weight, point, bias, tx, txt,
    su_s, su_r, mx_s, mx_r, sg_s, sg_r, ad_s, ad_r,
    du_r, dg_r, pt_r,
    f_sem, c_sem, i_sem, s_sem, r_sem, gs_sem, gr_sem, ps_sem, pr_sem,
):
    S, D, Y, C, XO, YW, Z, J = sizes
    A = S // Y
    X = A // 2
    CY = C * YW
    H = C // 2
    me = lax.axis_index("space")
    dp = lax.axis_index("dp")
    mine_x = me // (2 * Y)
    mine_y = lax.rem(me // 2, Y)
    mine_c = lax.rem(me, 2)

    def f_copy(x):
        return pltpu.make_async_copy(fields.at[0, :, x], f_v.at[x], f_sem.at[x])

    def c_copy(x):
        return pltpu.make_async_copy(cot.at[0, :, x], c_v.at[x], c_sem.at[x])

    small = [
        pltpu.make_async_copy(src, dst, i_sem.at[n])
        for n, (src, dst) in enumerate(
            [(tz_in, tz), (tx_in, tx), (txt_in, txt), (weight_in, weight),
             (point_in, point), (bias_in, bias)]
        )
    ]
    small[0].start()
    for x in range(XO):
        f_copy(x).start()

    def far_first(i):
        n, m = i // A, lax.rem(i // 2, X)
        step_y = Y + Y // 2 + ((n + 1) // 2) * (1 - 2 * lax.rem(n, 2))
        step_x = X + X // 2 + ((m + 1) // 2) * (1 - 2 * lax.rem(m, 2))
        to_x = lax.rem(mine_x + step_x, X)
        to_y = lax.rem(mine_y + step_y, Y)
        to_c = lax.rem(mine_c + 1 - lax.rem(i, 2), 2)
        return (to_x * Y + to_y) * 2 + to_c

    barrier = pltpu.get_barrier_semaphore()

    @pl.loop(0, S - 1)
    def _(i):
        pl.semaphore_signal(
            barrier, inc=1, device_id={"space": far_first(i)}, device_id_type=MESH
        )

    @pl.loop(1, D)
    def _(i):
        pl.semaphore_signal(
            barrier, inc=1, device_id={"dp": lax.rem(dp + i, D)}, device_id_type=MESH
        )

    for copy in small[1:]:
        copy.start()
    for x in range(XO):
        c_copy(x).start()

    def send_copy(n, src, dst, to):
        return pltpu.make_async_remote_copy(
            src_ref=src, dst_ref=dst, send_sem=s_sem.at[n], recv_sem=r_sem.at[n],
            device_id={"space": to}, device_id_type=MESH,
        )

    def scatter(n, sent, got):
        @pl.loop(0, S - 1)
        def _(i):
            to = far_first(i)
            send_copy(n, sent.at[to], got.at[me], to).start()

        got[pl.ds(me, 1)] = sent[pl.ds(me, 1)]

    def all_of(n, ref):
        some = ref.at[pl.ds(0, S - 1)]
        return send_copy(n, some, some, lax.rem(me + 1, S))

    def gather_copy(n, ref, to):
        return pltpu.make_async_remote_copy(
            src_ref=ref, dst_ref=ref, send_sem=gs_sem.at[n], recv_sem=gr_sem.at[n],
            device_id={"dp": to}, device_id_type=MESH,
        )

    def gather(n, ref, value):
        ref[pl.ds(dp, 1)] = value[None]

        @pl.loop(1, D)
        def _(i):
            gather_copy(n, ref.at[dp], lax.rem(dp + i, D)).start()

    def gather_all(n, ref):
        return gather_copy(n, ref.at[pl.ds(0, D - 1)], lax.rem(dp + 1, D))

    def rows_of(ref, x):
        return ref[x].reshape(CY, Z)

    small[0].wait()
    for x in range(XO):
        f_copy(x).wait()
        stage[pl.ds(x, S, stride=XO), :] = dot(tz[...], rows_of(f_v, x), 1, 1)
    su_s[...] = stage[...].reshape(S, XO, CY).astype(BF16)
    pl.semaphore_wait(barrier, S + D - 2)
    scatter(0, su_s, su_r)

    for copy in small[1:]:
        copy.wait()
    for c in range(C):
        w2[c] = jnp.concatenate([weight[c, :H, :], weight[c, H:, :]], axis=-1)
    spread = (
        lax.broadcasted_iota(jnp.int32, (CY, C), 0) // YW
        == lax.broadcasted_iota(jnp.int32, (CY, C), 1)
    )
    spread_f = spread.astype(F32)
    spread_b = spread.astype(BF16)
    same = (
        lax.broadcasted_iota(jnp.int32, (CY, CY), 0) % YW
        == lax.broadcasted_iota(jnp.int32, (CY, CY), 1) % YW
    )

    def kron(part, flip):
        rows = dot(spread_b, part, 1, 0 if not flip else 1).astype(BF16)
        return jnp.where(same, dot(rows, spread_b, 1, 1), 0.0).astype(BF16)

    p_high, p_low = split(point[...])
    into_out = jnp.concatenate([kron(p_high, True), kron(p_low, True)], axis=1)
    into_in = jnp.concatenate([kron(p_high, False), kron(p_low, False)], axis=1)
    bias_col = jnp.sum(spread_f * bias[...], axis=1, keepdims=True)

    for x in range(XO):
        rows = rows_of(f_v, x)
        acc_v[x] = dot(into_out, jnp.concatenate([rows, rows], axis=0), 1, 0) + bias_col

    lane = lax.broadcasted_iota(jnp.int32, (H, YW, 2 * J), 2)

    def spectrum(got):
        rows = got[...].reshape(S * XO, CY)
        return dot(tx[...], rows, 1, 0).T.reshape(C, YW, 2 * J)

    def back(values, sent):
        high, low = split(values)
        rows = dot(txt[...], jnp.concatenate([high, low], axis=1), 1, 1)
        sent[...] = rows.reshape(S, XO, CY).astype(BF16)

    all_of(0, su_r).wait_recv()
    spec_u = spectrum(su_r)
    mixed = []
    for o in range(H):
        total = w2[0, o : o + 1, :] * spec_u[0]
        for c in range(1, C):
            total = total + w2[c, o : o + 1, :] * spec_u[c]
        mixed.append(total[None])
    mixed = jnp.concatenate(mixed, axis=0)
    mixed = jnp.concatenate(
        [jnp.where(lane < J, mixed, 0.0), jnp.where(lane >= J, mixed, 0.0)], axis=0
    )
    back(mixed.reshape(CY, 2 * J), mx_s)
    scatter(1, mx_s, mx_r)
    gather(0, du_r, spec_u.astype(BF16))

    all_of(1, mx_r).wait_recv()
    stage[...] = mx_r[...].astype(F32).reshape(S * XO, CY)
    for x in range(XO):
        c_copy(x).wait()

    def slope_step(x, bias_sum):
        modes = stage[pl.ds(x, S, stride=XO), :].T.astype(BF16)
        pre = acc_v[x] + dot(modes, tz[...], 1, 0)
        grad = (rows_of(c_v, x).astype(F32) * gelu_slope(pre)).astype(BF16)
        g_v[x] = grad
        depth = dot(tz[...], grad, 1, 1)
        stage[pl.ds(x, S, stride=XO), :] = depth
        return bias_sum + depth[0:1, :]

    bias_sum = jnp.zeros((1, CY), F32)
    for x in range(XO):
        bias_sum = slope_step(x, bias_sum)
    sg_s[...] = stage[...].reshape(S, XO, CY).astype(BF16)
    scatter(2, sg_s, sg_r)

    pairs = jnp.zeros((CY, CY), F32)
    for x in range(XO):
        pairs = pairs + dot(rows_of(f_v, x), g_v[x], 1, 1)
    pairs = jnp.sum(jnp.where(same, pairs, 0.0).reshape(C, YW, CY), axis=1)
    constant = float(np.float32(ml_dtypes.bfloat16(math.sqrt(1.0 / Z))))
    terms = jnp.concatenate(
        [pairs[:H], pairs[H:], jnp.broadcast_to(bias_sum * (1.0 / constant), (H, CY))], axis=1
    )
    source = lax.broadcasted_iota(jnp.int32, (3 * CY, 128), 0)
    fold = (source // CY) * C + (source % CY) // YW == lax.broadcasted_iota(
        jnp.int32, (3 * CY, 128), 1
    )
    tile = dot(terms, fold.astype(F32), 1, 0, precision=lax.Precision.HIGHEST)

    mine_a = mine_x * 2 + mine_c

    def to_a(a):
        return {"space": ((a // 2) * Y + mine_y) * 2 + lax.rem(a, 2)}

    def to_y(y):
        return {"space": (mine_x * Y + y) * 2 + mine_c}

    def to_dp(d):
        return {"dp": d}

    rounds = [(0, A, mine_a, to_a, 0), (1, Y, mine_y, to_y, A), (2, D, dp, to_dp, A + Y)]

    def p_copy(n, first, last, place):
        return pltpu.make_async_remote_copy(
            src_ref=first, dst_ref=last, send_sem=ps_sem.at[n], recv_sem=pr_sem.at[n],
            device_id=place, device_id_type=MESH,
        )

    def p_send(n, value):
        _, count, mine, place, base = rounds[n]
        pt_r[pl.ds(base + mine, 1)] = value[None]

        @pl.loop(1, count)
        def _(i):
            slot = pt_r.at[base + mine]
            p_copy(n, slot, slot, place(lax.rem(mine + i, count))).start()

    def p_all(n):
        _, count, mine, place, base = rounds[n]
        some = pt_r.at[pl.ds(base, count - 1)]
        return p_copy(n, some, some, place(lax.rem(mine + 1, count)))

    def p_sum(n):
        _, count, _, _, base = rounds[n]
        p_all(n).wait_recv()
        total = pt_r[base]
        for i in range(1, count):
            total = total + pt_r[base + i]
        return total

    p_send(0, tile)
    for x in range(XO):
        rows = g_v[x]
        acc_v[x] = dot(into_in, jnp.concatenate([rows, rows], axis=0), 1, 0)
    gather_all(0, du_r).wait_recv()
    su_out[...] = du_r[...]
    p_send(1, p_sum(0))

    all_of(2, sg_r).wait_recv()
    spec = spectrum(sg_r)
    pair = jnp.where(lane < J, spec[:H], spec[H:])
    adjoint = []
    for c in range(C):
        total = w2[c, 0:1, :] * pair[0]
        for o in range(1, H):
            total = total + w2[c, o : o + 1, :] * pair[o]
        adjoint.append(total[None])
    back(jnp.concatenate(adjoint, axis=0).reshape(CY, 2 * J), ad_s)
    scatter(3, ad_s, ad_r)
    gather(1, dg_r, pair.astype(BF16))
    p_send(2, p_sum(1))

    all_of(3, ad_r).wait_recv()
    ad_out[...] = ad_r[...]
    gather_all(1, dg_r).wait_recv()
    sg_out[...] = dg_r[...]
    sum_out[...] = p_sum(2)

    all_of(0, su_s).wait_send()
    all_of(1, mx_s).wait_send()
    all_of(2, sg_s).wait_send()
    all_of(3, ad_s).wait_send()
    for n in range(3):
        p_all(n).wait_send()
    gather_all(0, du_r).wait_send()
    gather_all(1, dg_r).wait_send()


def result_kernel(
    sizes, acc, ad, su, sg, sums, tz,
    out, gm_out, gp_out, gb_out,
    out_v, stage, sg_v, gm_v, gp_v, gb_v, o_sem, g_sem,
):
    S, D, Y, C, XO, YW, Z, J = sizes
    CY = C * YW
    H = C // 2

    def o_copy(x):
        return pltpu.make_async_copy(out_v.at[x], out.at[0, :, x], o_sem.at[x])

    stage[...] = ad[...].astype(F32).reshape(S * XO, CY)
    for x in range(XO):
        modes = stage[pl.ds(x, S, stride=XO), :].T.astype(BF16)
        grad = acc[x] + dot(modes, tz[...], 1, 0)
        out_v[x] = grad.astype(BF16).reshape(C, YW, Z)
        o_copy(x).start()

    final = sums[...] * (1.0 / math.sqrt(D * S * XO * YW * Z))
    gp_v[...] = jnp.concatenate([final[:, :C], final[:, C : 2 * C]], axis=0)
    gb_v[...] = final[0:1, 2 * C : 3 * C]
    sg_v[...] = sg[...].astype(F32) * (1.0 / math.sqrt(D * YW))
    for c in range(C):
        total = su[0, c].astype(F32)[None] * sg_v[0]
        for d in range(1, D):
            total = total + su[d, c].astype(F32)[None] * sg_v[d]
        total = jnp.sum(total, axis=1)
        gm_v[c, :H, :] = total[:, :J]
        gm_v[c, H:, :] = total[:, J:]
    copies = [
        pltpu.make_async_copy(src, dst, g_sem.at[n])
        for n, (src, dst) in enumerate([(gm_v, gm_out), (gp_v, gp_out), (gb_v, gb_out)])
    ]
    for copy in copies:
        copy.start()
    for x in range(XO):
        o_copy(x).wait()
    for copy in copies:
        copy.wait()


def shards(S, D, fields, cotangent, mode_weight, point_weight, bias_vector):
    _, C, XO, YW, Z = fields.shape
    J = mode_weight.shape[2]
    CY = C * YW
    Y = 8 if S == 64 else 2
    A = S // Y
    H = C // 2
    tz = basis_table(S, Z)
    tx = basis_table(J, S * XO)
    tx = np.concatenate([tx, tx], axis=0)
    txt = np.ascontiguousarray(np.concatenate([tx, tx], axis=0).T)
    sizes = (S, D, Y, C, XO, YW, Z, J)
    block = (S, XO, CY)
    vmem = pl.BlockSpec(memory_space=pltpu.VMEM)
    hbm = pl.BlockSpec(memory_space=pltpu.HBM)
    dma = pltpu.SemaphoreType.DMA
    shape = jax.ShapeDtypeStruct
    held = pl.pallas_call(
        functools.partial(layer_kernel, sizes),
        out_shape=(
            shape((XO, CY, Z), F32),
            shape(block, BF16),
            shape((D, C, YW, 2 * J), BF16),
            shape((D, H, YW, 2 * J), BF16),
            shape((H, 128), F32),
            shape((S, Z), BF16),
        ),
        in_specs=[hbm] * 8,
        out_specs=(vmem,) * 6,
        scratch_shapes=[
            pltpu.VMEM((XO, C, YW, Z), BF16),
            pltpu.VMEM((XO, C, YW, Z), BF16),
            pltpu.VMEM((XO, CY, Z), BF16),
            pltpu.VMEM((S * XO, CY), F32),
            pltpu.VMEM((C, H, 2 * J), F32),
            pltpu.VMEM((C, C, J), F32),
            pltpu.VMEM((C, C), F32),
            pltpu.VMEM((1, C), F32),
            pltpu.VMEM((2 * J, S * XO), BF16),
            pltpu.VMEM((S * XO, 4 * J), BF16),
        ]
        + [pltpu.VMEM(block, BF16)] * 8
        + [
            pltpu.VMEM((D, C, YW, 2 * J), BF16),
            pltpu.VMEM((D, H, YW, 2 * J), BF16),
            pltpu.VMEM((A + Y + D, H, 128), F32),
            dma((XO,)),
            dma((XO,)),
            dma((6,)),
            dma((4,)),
            dma((4,)),
            dma((2,)),
            dma((2,)),
            dma((3,)),
            dma((3,)),
        ],
        compiler_params=pltpu.CompilerParams(
            collective_id=0, has_side_effects=True, vmem_limit_bytes=24 * 1024 * 1024
        ),
    )(
        *(
            pltpu.with_memory_space_constraint(operand, pltpu.HBM)
            for operand in (
                fields,
                cotangent,
                mode_weight.reshape(C, C, J),
                point_weight,
                bias_vector.reshape(1, C),
                jnp.asarray(tz),
                jnp.asarray(tx),
                jnp.asarray(txt),
            )
        )
    )
    grad_fields, grad_mode, grad_point, grad_bias = pl.pallas_call(
        functools.partial(result_kernel, sizes),
        out_shape=(
            shape(fields.shape, BF16),
            shape((C, C, J), F32),
            shape((C, C), F32),
            shape((1, C), F32),
        ),
        in_specs=[vmem] * 6,
        out_specs=(hbm,) * 4,
        scratch_shapes=[
            pltpu.VMEM((XO, C, YW, Z), BF16),
            pltpu.VMEM((S * XO, CY), F32),
            pltpu.VMEM((D, H, YW, 2 * J), F32),
            pltpu.VMEM((C, C, J), F32),
            pltpu.VMEM((C, C), F32),
            pltpu.VMEM((1, C), F32),
            dma((XO,)),
            dma((3,)),
        ],
        compiler_params=pltpu.CompilerParams(vmem_limit_bytes=24 * 1024 * 1024),
    )(*held)
    return (
        grad_fields,
        grad_mode.reshape(mode_weight.shape),
        grad_point,
        grad_bias.reshape(C),
    )


def solution(mesh):
    return jax.shard_map(
        functools.partial(shards, mesh.shape["space"], mesh.shape["dp"]),
        mesh=mesh,
        in_specs=(
            P("dp", None, "space", None, None),
            P("dp", None, "space", None, None),
            P(None, None, None, "space"),
            P(),
            P(),
        ),
        out_specs=(P("dp", None, "space", None, None), P(None, None, None, "space"), P(), P()),
        check_vma=False,
    )
```

time: 67 us -> 52.9 us (0.79); the launches traced: 66.1 us -> 52.8 us
  local copies, waits for them, and re-layouts: 10.1 us -> 0 us
  Pallas kernels: 55.4 us -> 52.2 us
    unnamed x20 -> x0, local copies, waits for them, and re-layouts: 10.1 us -> none
    pallas_call x1 -> x2, Pallas kernels: 55.4 us -> 52.2 us  [the longest x1 50.5 us: shards(): pl.pallas_call(functools.partial(layer_kernel, sizes), out_shape=(shape((...]
where the time goes in v1:
time: 52.9 us; the launch traced here: 52.8 us
  Pallas kernels  52.2 us (99%)
  between operations  0.64 us (1%)
    pallas_call x1, Pallas kernels, shards(): pl.pallas_call(functools.partial(layer_kernel, sizes), out_shape=(shape((...  50.5 us
    pallas_call x1, Pallas kernels, shards(): pl.pallas_call(functools.partial(result_kernel, sizes), out_shape=(shape(...  1.65 us

profile of v1, /device:TPU:1, one launch (start us, length us, event | category | flops | bytes accessed | tf_op | source)
XLA Modules:
  0.0 52.8 jit_solution(11040792578528787510)
XLA Ops:
  0.6 50.5 %shard_map.111 = (f32[8,128,512]{2,1,0:T(8,128)S(1)}, bf16[64,8,128]{2,1,0:T(8,128)(2,1)S(1)}, bf16[8,16,8,128]{3,2,1,0:T(8,128)(2,1)S(1)}, bf16[8,8,8,128]{3,2,...) custom-call(bf16[1,16,8,8,512]{4,3,2,1,0:T(8,128)(2,1)} %fields.1, ...), custom_call_target="tpu_custom_call" | custom-call | tf_op jit(solution)/shard_map/pallas_call | solution.py:383
  51.2 1.7 %shard_map.112 = (bf16[1,16,8,8,512]{4,3,2,1,0:T(8,128)(2,1)}, f32[16,16,64]{2,1,0:T(8,128)}, f32[16,16]{1,0:T(8,128)}, f32[1,16]{1,0:T(1,128)}) custom-call(f32[8,128,512]{2,1,0:T(8,128)S(1)} %get-tuple-element.14.acc, bf16[64,8,128]{2,1,0:T(8,128)(2,1)S(1)} %get-tuple-element.15.ad, bf16[8,16,8,128]{3,2,1,0:T(8,128)(2,1)S(1)} %get-tuple-element.16.su, ...), custom_call_target="tpu_custom_call" | custom-call | tf_op jit(solution)/shard_map/pallas_call | solution.py:440

commit v2 on v1

--- a/solution.py
+++ b/solution.py
@@ -52,9 +52,10 @@
     du_r, dg_r, pt_r,
     f_sem, c_sem, i_sem, s_sem, r_sem, gs_sem, gr_sem, ps_sem, pr_sem,
 ):
-    S, D, Y, C, XO, YW, Z, J = sizes
+    S, D, Y, C, XO, YW, Z, J, Q = sizes
     A = S // Y
     X = A // 2
+    R = XO // Q
     CY = C * YW
     H = C // 2
     me = lax.axis_index("space")
@@ -80,22 +81,26 @@
     for x in range(XO):
         f_copy(x).start()
 
-    def far_first(i):
-        n, m = i // A, lax.rem(i // 2, X)
-        step_y = Y + Y // 2 + ((n + 1) // 2) * (1 - 2 * lax.rem(n, 2))
-        step_x = X + X // 2 + ((m + 1) // 2) * (1 - 2 * lax.rem(m, 2))
-        to_x = lax.rem(mine_x + step_x, X)
-        to_y = lax.rem(mine_y + step_y, Y)
-        to_c = lax.rem(mine_c + 1 - lax.rem(i, 2), 2)
-        return (to_x * Y + to_y) * 2 + to_c
+    def far_first(act):
+        classes = [(a, b) for a in range(X // 2 + 1) for b in range(Y // 2 + 1)]
+        for a, b in sorted(classes, key=lambda hops: -sum(hops)):
+            ways_x = 1 if 2 * a % X == 0 else 2
+            ways_y = 1 if 2 * b % Y == 0 else 2
+
+            @pl.loop(0, 2 * ways_x * ways_y if a + b else 1)
+            def _(i):
+                turn_x = lax.rem(i // 2, ways_x)
+                turn_y = i // (2 * ways_x)
+                to_x = lax.rem(mine_x + a + turn_x * (X - 2 * a), X)
+                to_y = lax.rem(mine_y + b + turn_y * (Y - 2 * b), Y)
+                to_c = lax.rem(mine_c + 1 + lax.rem(i, 2), 2)
+                act((to_x * Y + to_y) * 2 + to_c)
 
     barrier = pltpu.get_barrier_semaphore()
 
-    @pl.loop(0, S - 1)
-    def _(i):
-        pl.semaphore_signal(
-            barrier, inc=1, device_id={"space": far_first(i)}, device_id_type=MESH
-        )
+    @far_first
+    def _(to):
+        pl.semaphore_signal(barrier, inc=1, device_id={"space": to}, device_id_type=MESH)
 
     @pl.loop(1, D)
     def _(i):
@@ -114,17 +119,16 @@
             device_id={"space": to}, device_id_type=MESH,
         )
 
-    def scatter(n, sent, got):
-        @pl.loop(0, S - 1)
-        def _(i):
-            to = far_first(i)
-            send_copy(n, sent.at[to], got.at[me], to).start()
-
-        got[pl.ds(me, 1)] = sent[pl.ds(me, 1)]
-
-    def all_of(n, ref):
-        some = ref.at[pl.ds(0, S - 1)]
-        return send_copy(n, some, some, lax.rem(me + 1, S))
+    def scatter(n, q, sent, got):
+        @far_first
+        def _(to):
+            send_copy(n * Q + q, sent.at[q, to], got.at[q, me], to).start()
+
+        got[q, pl.ds(me, 1)] = sent[q, pl.ds(me, 1)]
+
+    def all_of(n, q, ref):
+        some = ref.at[q, pl.ds(0, S - 1)]
+        return send_copy(n * Q + q, some, some, lax.rem(me + 1, S))
 
     def gather_copy(n, ref, to):
         return pltpu.make_async_remote_copy(
@@ -146,12 +150,14 @@
         return ref[x].reshape(CY, Z)
 
     small[0].wait()
-    for x in range(XO):
-        f_copy(x).wait()
-        stage[pl.ds(x, S, stride=XO), :] = dot(tz[...], rows_of(f_v, x), 1, 1)
-    su_s[...] = stage[...].reshape(S, XO, CY).astype(BF16)
-    pl.semaphore_wait(barrier, S + D - 2)
-    scatter(0, su_s, su_r)
+    for q in range(Q):
+        for r in range(R):
+            f_copy(q * R + r).wait()
+            stage[q, pl.ds(r, S, stride=R), :] = dot(tz[...], rows_of(f_v, q * R + r), 1, 1)
+        su_s[q] = stage[q].astype(BF16).reshape(S, R, CY)
+        if q == 0:
+            pl.semaphore_wait(barrier, S + D - 2)
+        scatter(0, q, su_s, su_r)
 
     for copy in small[1:]:
         copy.wait()
@@ -184,15 +190,16 @@
     lane = lax.broadcasted_iota(jnp.int32, (H, YW, 2 * J), 2)
 
     def spectrum(got):
-        rows = got[...].reshape(S * XO, CY)
+        rows = got[...].reshape(Q * S * R, CY)
         return dot(tx[...], rows, 1, 0).T.reshape(C, YW, 2 * J)
 
-    def back(values, sent):
+    def back(values):
         high, low = split(values)
         rows = dot(txt[...], jnp.concatenate([high, low], axis=1), 1, 1)
-        sent[...] = rows.reshape(S, XO, CY).astype(BF16)
-
-    all_of(0, su_r).wait_recv()
+        return rows.astype(BF16).reshape(Q, S, R, CY)
+
+    for q in range(Q):
+        all_of(0, q, su_r).wait_recv()
     spec_u = spectrum(su_r)
     mixed = []
     for o in range(H):
@@ -204,29 +211,29 @@
     mixed = jnp.concatenate(
         [jnp.where(lane < J, mixed, 0.0), jnp.where(lane >= J, mixed, 0.0)], axis=0
     )
-    back(mixed.reshape(CY, 2 * J), mx_s)
-    scatter(1, mx_s, mx_r)
-    gather(0, du_r, spec_u.astype(BF16))
-
-    all_of(1, mx_r).wait_recv()
-    stage[...] = mx_r[...].astype(F32).reshape(S * XO, CY)
-    for x in range(XO):
-        c_copy(x).wait()
-
-    def slope_step(x, bias_sum):
-        modes = stage[pl.ds(x, S, stride=XO), :].T.astype(BF16)
-        pre = acc_v[x] + dot(modes, tz[...], 1, 0)
-        grad = (rows_of(c_v, x).astype(F32) * gelu_slope(pre)).astype(BF16)
-        g_v[x] = grad
-        depth = dot(tz[...], grad, 1, 1)
-        stage[pl.ds(x, S, stride=XO), :] = depth
-        return bias_sum + depth[0:1, :]
+    mx_s[...] = back(mixed.reshape(CY, 2 * J))
+    for q in range(Q):
+        scatter(1, q, mx_s, mx_r)
+    gather(0, du_r, jnp.where(lane < J, spec_u[:H], spec_u[H:]).astype(BF16))
 
     bias_sum = jnp.zeros((1, CY), F32)
-    for x in range(XO):
-        bias_sum = slope_step(x, bias_sum)
-    sg_s[...] = stage[...].reshape(S, XO, CY).astype(BF16)
-    scatter(2, sg_s, sg_r)
+    for q in range(Q):
+        all_of(1, q, mx_r).wait_recv()
+        stage[q] = mx_r[q].reshape(S * R, CY).astype(F32)
+        if q == 0:
+            for x in range(XO):
+                c_copy(x).wait()
+        for r in range(R):
+            x = q * R + r
+            modes = stage[q, pl.ds(r, S, stride=R), :].T.astype(BF16)
+            pre = acc_v[x] + dot(modes, tz[...], 1, 0)
+            grad = (rows_of(c_v, x).astype(F32) * gelu_slope(pre)).astype(BF16)
+            g_v[x] = grad
+            depth = dot(tz[...], grad, 1, 1)
+            stage[q, pl.ds(r, S, stride=R), :] = depth
+            bias_sum = bias_sum + depth[0:1, :]
+        sg_s[q] = stage[q].astype(BF16).reshape(S, R, CY)
+        scatter(2, q, sg_s, sg_r)
 
     pairs = jnp.zeros((CY, CY), F32)
     for x in range(XO):
@@ -291,30 +298,32 @@
     su_out[...] = du_r[...]
     p_send(1, p_sum(0))
 
-    all_of(2, sg_r).wait_recv()
+    for q in range(Q):
+        all_of(2, q, sg_r).wait_recv()
     spec = spectrum(sg_r)
     pair = jnp.where(lane < J, spec[:H], spec[H:])
+    gather(1, dg_r, pair.astype(BF16))
     adjoint = []
     for c in range(C):
         total = w2[c, 0:1, :] * pair[0]
         for o in range(1, H):
             total = total + w2[c, o : o + 1, :] * pair[o]
         adjoint.append(total[None])
-    back(jnp.concatenate(adjoint, axis=0).reshape(CY, 2 * J), ad_s)
-    scatter(3, ad_s, ad_r)
-    gather(1, dg_r, pair.astype(BF16))
+    ad_s[...] = back(jnp.concatenate(adjoint, axis=0).reshape(CY, 2 * J))
+    for q in range(Q):
+        scatter(3, q, ad_s, ad_r)
     p_send(2, p_sum(1))
 
-    all_of(3, ad_r).wait_recv()
+    for q in range(Q):
+        all_of(3, q, ad_r).wait_recv()
     ad_out[...] = ad_r[...]
     gather_all(1, dg_r).wait_recv()
     sg_out[...] = dg_r[...]
     sum_out[...] = p_sum(2)
 
-    all_of(0, su_s).wait_send()
-    all_of(1, mx_s).wait_send()
-    all_of(2, sg_s).wait_send()
-    all_of(3, ad_s).wait_send()
+    for q in range(Q):
+        for n, sent in enumerate([su_s, mx_s, sg_s, ad_s]):
+            all_of(n, q, sent).wait_send()
     for n in range(3):
         p_all(n).wait_send()
     gather_all(0, du_r).wait_send()
@@ -326,16 +335,18 @@
     out, gm_out, gp_out, gb_out,
     out_v, stage, sg_v, gm_v, gp_v, gb_v, o_sem, g_sem,
 ):
-    S, D, Y, C, XO, YW, Z, J = sizes
+    S, D, Y, C, XO, YW, Z, J, Q = sizes
     CY = C * YW
     H = C // 2
+    R = XO // Q
+    low = lax.broadcasted_iota(jnp.int32, (YW, 2 * J), 1) < J
 
     def o_copy(x):
         return pltpu.make_async_copy(out_v.at[x], out.at[0, :, x], o_sem.at[x])
 
-    stage[...] = ad[...].astype(F32).reshape(S * XO, CY)
-    for x in range(XO):
-        modes = stage[pl.ds(x, S, stride=XO), :].T.astype(BF16)
+    stage[...] = ad[...].reshape(Q, S * R, CY).astype(F32)
+    for x in range(XO):
+        modes = stage[x // R, pl.ds(x % R, S, stride=R), :].T.astype(BF16)
         grad = acc[x] + dot(modes, tz[...], 1, 0)
         out_v[x] = grad.astype(BF16).reshape(C, YW, Z)
         o_copy(x).start()
@@ -345,9 +356,12 @@
     gb_v[...] = final[0:1, 2 * C : 3 * C]
     sg_v[...] = sg[...].astype(F32) * (1.0 / math.sqrt(D * YW))
     for c in range(C):
-        total = su[0, c].astype(F32)[None] * sg_v[0]
-        for d in range(1, D):
-            total = total + su[d, c].astype(F32)[None] * sg_v[d]
+        total = 0.0
+        for d in range(D):
+            both = su[d, c % H].astype(F32)
+            turned = pltpu.roll(both, J, 1)
+            both = jnp.where(low, both, turned) if c < H else jnp.where(low, turned, both)
+            total = total + both[None] * sg_v[d]
         total = jnp.sum(total, axis=1)
         gm_v[c, :H, :] = total[:, :J]
         gm_v[c, H:, :] = total[:, J:]
@@ -371,11 +385,13 @@
     A = S // Y
     H = C // 2
     tz = basis_table(S, Z)
-    tx = basis_table(J, S * XO)
+    Q = 1
+    R = XO // Q
+    tx = basis_table(J, S * XO).reshape(J, S, Q, R).swapaxes(1, 2).reshape(J, S * XO)
     tx = np.concatenate([tx, tx], axis=0)
     txt = np.ascontiguousarray(np.concatenate([tx, tx], axis=0).T)
-    sizes = (S, D, Y, C, XO, YW, Z, J)
-    block = (S, XO, CY)
+    sizes = (S, D, Y, C, XO, YW, Z, J, Q)
+    block = (Q, S, R, CY)
     vmem = pl.BlockSpec(memory_space=pltpu.VMEM)
     hbm = pl.BlockSpec(memory_space=pltpu.HBM)
     dma = pltpu.SemaphoreType.DMA
@@ -385,7 +401,7 @@
         out_shape=(
             shape((XO, CY, Z), F32),
             shape(block, BF16),
-            shape((D, C, YW, 2 * J), BF16),
+            shape((D, H, YW, 2 * J), BF16),
             shape((D, H, YW, 2 * J), BF16),
             shape((H, 128), F32),
             shape((S, Z), BF16),
@@ -396,7 +412,7 @@
             pltpu.VMEM((XO, C, YW, Z), BF16),
             pltpu.VMEM((XO, C, YW, Z), BF16),
             pltpu.VMEM((XO, CY, Z), BF16),
-            pltpu.VMEM((S * XO, CY), F32),
+            pltpu.VMEM((Q, S * R, CY), F32),
             pltpu.VMEM((C, H, 2 * J), F32),
             pltpu.VMEM((C, C, J), F32),
             pltpu.VMEM((C, C), F32),
@@ -406,14 +422,14 @@
         ]
         + [pltpu.VMEM(block, BF16)] * 8
         + [
-            pltpu.VMEM((D, C, YW, 2 * J), BF16),
+            pltpu.VMEM((D, H, YW, 2 * J), BF16),
             pltpu.VMEM((D, H, YW, 2 * J), BF16),
             pltpu.VMEM((A + Y + D, H, 128), F32),
             dma((XO,)),
             dma((XO,)),
             dma((6,)),
-            dma((4,)),
-            dma((4,)),
+            dma((4 * Q,)),
+            dma((4 * Q,)),
             dma((2,)),
             dma((2,)),
             dma((3,)),
@@ -449,7 +465,7 @@
         out_specs=(hbm,) * 4,
         scratch_shapes=[
             pltpu.VMEM((XO, C, YW, Z), BF16),
-            pltpu.VMEM((S * XO, CY), F32),
+            pltpu.VMEM((Q, S * R, CY), F32),
             pltpu.VMEM((D, H, YW, 2 * J), F32),
             pltpu.VMEM((C, C, J), F32),
             pltpu.VMEM((C, C), F32),

time: 52.9 us -> 49 us (0.926)
  Pallas kernels: 52.2 us -> 48.2 us
    pallas_call x1, Pallas kernels: 50.5 us -> 46.4 us  [shards(): pl.pallas_call(functools.partial(layer_kernel, sizes), out_shape=(shape((...]
where the time goes in v2:
time: 49 us; the launch traced here: 48.9 us
  Pallas kernels  48.2 us (98%)
  between operations  0.64 us (1%)
    pallas_call x1, Pallas kernels, shards(): pl.pallas_call(functools.partial(layer_kernel, sizes), out_shape=(shape((...  46.4 us
    pallas_call x1, Pallas kernels, shards(): pl.pallas_call(functools.partial(result_kernel, sizes), out_shape=(shape(...  1.87 us

profile of v2, /device:TPU:1, one launch (start us, length us, event | category | flops | bytes accessed | tf_op | source)
XLA Modules:
  0.0 48.9 jit_solution(14068269036362939783)
XLA Ops:
  0.6 46.4 %shard_map.111 = (f32[8,128,512]{2,1,0:T(8,128)S(1)}, bf16[1,64,8,128]{3,2,1,0:T(8,128)(2,1)S(1)}, bf16[8,8,8,128]{3,2,1,0:T(8,128)(2,1)S(1)}, bf16[8,8,8,128]{3...) custom-call(bf16[1,16,8,8,512]{4,3,2,1,0:T(8,128)(2,1)} %fields.1, ...), custom_call_target="tpu_custom_call" | custom-call | tf_op jit(solution)/shard_map/pallas_call | solution.py:399
  47.0 1.9 %shard_map.112 = (bf16[1,16,8,8,512]{4,3,2,1,0:T(8,128)(2,1)}, f32[16,16,64]{2,1,0:T(8,128)}, f32[16,16]{1,0:T(8,128)}, f32[1,16]{1,0:T(1,128)}) custom-call(f32[8,128,512]{2,1,0:T(8,128)S(1)} %get-tuple-element.14.acc, bf16[1,64,8,128]{3,2,1,0:T(8,128)(2,1)S(1)} %get-tuple-element.15.ad, bf16[8,8,8,128]{3,2,1,0:T(8,128)(2,1)S(1)} %get-tuple-element.16.su, ...), custom_call_target="tpu_custom_call" | custom-call | tf_op jit(solution)/shard_map/pallas_call | solution.py:456

commit v3 on v2

--- a/solution.py
+++ b/solution.py
@@ -77,10 +77,6 @@
              (point_in, point), (bias_in, bias)]
         )
     ]
-    small[0].start()
-    for x in range(XO):
-        f_copy(x).start()
-
     def far_first(act):
         classes = [(a, b) for a in range(X // 2 + 1) for b in range(Y // 2 + 1)]
         for a, b in sorted(classes, key=lambda hops: -sum(hops)):
@@ -93,8 +89,7 @@
                 turn_y = i // (2 * ways_x)
                 to_x = lax.rem(mine_x + a + turn_x * (X - 2 * a), X)
                 to_y = lax.rem(mine_y + b + turn_y * (Y - 2 * b), Y)
-                to_c = lax.rem(mine_c + 1 + lax.rem(i, 2), 2)
-                act((to_x * Y + to_y) * 2 + to_c)
+                act((to_x * Y + to_y) * 2 + lax.rem(i, 2) if a + b else me + 1 - 2 * mine_c)
 
     barrier = pltpu.get_barrier_semaphore()
 
@@ -108,6 +103,10 @@
             barrier, inc=1, device_id={"dp": lax.rem(dp + i, D)}, device_id_type=MESH
         )
 
+    small[0].start()
+    for x in range(XO):
+        f_copy(x).start()
+
     for copy in small[1:]:
         copy.start()
     for x in range(XO):
@@ -139,9 +138,10 @@
     def gather(n, ref, value):
         ref[pl.ds(dp, 1)] = value[None]
 
-        @pl.loop(1, D)
+        @pl.loop(0, D - 1)
         def _(i):
-            gather_copy(n, ref.at[dp], lax.rem(dp + i, D)).start()
+            step = D + D // 2 + ((i + 1) // 2) * (1 - 2 * lax.rem(i, 2))
+            gather_copy(n, ref.at[dp], lax.rem(dp + step, D)).start()
 
     def gather_all(n, ref):
         return gather_copy(n, ref.at[pl.ds(0, D - 1)], lax.rem(dp + 1, D))
@@ -151,9 +151,14 @@
 
     small[0].wait()
     for q in range(Q):
-        for r in range(R):
-            f_copy(q * R + r).wait()
-            stage[q, pl.ds(r, S, stride=R), :] = dot(tz[...], rows_of(f_v, q * R + r), 1, 1)
+        for r in range(0, R, 2):
+            x = q * R + r
+            f_copy(x).wait()
+            f_copy(x + 1).wait()
+            rows = jnp.concatenate([rows_of(f_v, x), rows_of(f_v, x + 1)], axis=0)
+            depth = dot(tz[...], rows, 1, 1)
+            for t in range(2):
+                stage[q, pl.ds(r + t, S, stride=R), :] = depth[:, t * CY : (t + 1) * CY]
         su_s[q] = stage[q].astype(BF16).reshape(S, R, CY)
         if q == 0:
             pl.semaphore_wait(barrier, S + D - 2)
@@ -226,12 +231,17 @@
         for r in range(R):
             x = q * R + r
             modes = stage[q, pl.ds(r, S, stride=R), :].T.astype(BF16)
-            pre = acc_v[x] + dot(modes, tz[...], 1, 0)
-            grad = (rows_of(c_v, x).astype(F32) * gelu_slope(pre)).astype(BF16)
-            g_v[x] = grad
-            depth = dot(tz[...], grad, 1, 1)
-            stage[q, pl.ds(r, S, stride=R), :] = depth
-            bias_sum = bias_sum + depth[0:1, :]
+            acc_v[x] = acc_v[x] + dot(modes, tz[...], 1, 0)
+        for r in range(R):
+            x = q * R + r
+            g_v[x] = (rows_of(c_v, x).astype(F32) * gelu_slope(acc_v[x])).astype(BF16)
+        for r in range(0, R, 2):
+            x = q * R + r
+            depth = dot(tz[...], jnp.concatenate([g_v[x], g_v[x + 1]], axis=0), 1, 1)
+            for t in range(2):
+                part = depth[:, t * CY : (t + 1) * CY]
+                stage[q, pl.ds(r + t, S, stride=R), :] = part
+                bias_sum = bias_sum + part[0:1, :]
         sg_s[q] = stage[q].astype(BF16).reshape(S, R, CY)
         scatter(2, q, sg_s, sg_r)
 
@@ -294,9 +304,15 @@
     for x in range(XO):
         rows = g_v[x]
         acc_v[x] = dot(into_in, jnp.concatenate([rows, rows], axis=0), 1, 0)
+    p_send(1, p_sum(0))
     gather_all(0, du_r).wait_recv()
-    su_out[...] = du_r[...]
-    p_send(1, p_sum(0))
+    low = lane[0] < J
+    for d in range(D):
+        for c in range(H):
+            both = du_r[d, c].astype(F32)
+            turned = pltpu.roll(both, J, 1)
+            su_out[d, c] = jnp.where(low, both, turned)
+            su_out[d, H + c] = jnp.where(low, turned, both)
 
     for q in range(Q):
         all_of(2, q, sg_r).wait_recv()
@@ -339,7 +355,6 @@
     CY = C * YW
     H = C // 2
     R = XO // Q
-    low = lax.broadcasted_iota(jnp.int32, (YW, 2 * J), 1) < J
 
     def o_copy(x):
         return pltpu.make_async_copy(out_v.at[x], out.at[0, :, x], o_sem.at[x])
@@ -358,10 +373,7 @@
     for c in range(C):
         total = 0.0
         for d in range(D):
-            both = su[d, c % H].astype(F32)
-            turned = pltpu.roll(both, J, 1)
-            both = jnp.where(low, both, turned) if c < H else jnp.where(low, turned, both)
-            total = total + both[None] * sg_v[d]
+            total = total + su[d, c][None] * sg_v[d]
         total = jnp.sum(total, axis=1)
         gm_v[c, :H, :] = total[:, :J]
         gm_v[c, H:, :] = total[:, J:]
@@ -401,7 +413,7 @@
         out_shape=(
             shape((XO, CY, Z), F32),
             shape(block, BF16),
-            shape((D, H, YW, 2 * J), BF16),
+            shape((D, C, YW, 2 * J), F32),
             shape((D, H, YW, 2 * J), BF16),
             shape((H, 128), F32),
             shape((S, Z), BF16),

time: 49 us -> 48 us (0.980)
  Pallas kernels: 48.2 us -> 47.2 us
    pallas_call x1, Pallas kernels: 46.4 us -> 45.6 us  [shards(): pl.pallas_call(functools.partial(layer_kernel, sizes), out_shape=(shape((...]
where the time goes in v3:
time: 48 us; the launch traced here: 47.9 us
  Pallas kernels  47.2 us (98%)
  between operations  0.64 us (1%)
    pallas_call x1, Pallas kernels, shards(): pl.pallas_call(functools.partial(layer_kernel, sizes), out_shape=(shape((...  45.6 us
    pallas_call x1, Pallas kernels, shards(): pl.pallas_call(functools.partial(result_kernel, sizes), out_shape=(shape(...  1.65 us

profile of v3, /device:TPU:1, one launch (start us, length us, event | category | flops | bytes accessed | tf_op | source)
XLA Modules:
  0.0 47.9 jit_solution(6560950506198187535)
XLA Ops:
  0.6 45.6 %shard_map.111 = (f32[8,128,512]{2,1,0:T(8,128)S(1)}, bf16[1,64,8,128]{3,2,1,0:T(8,128)(2,1)S(1)}, f32[8,16,8,128]{3,2,1,0:T(8,128)S(1)}, bf16[8,8,8,128]{3,2,1,...) custom-call(bf16[1,16,8,8,512]{4,3,2,1,0:T(8,128)(2,1)} %fields.1, ...), custom_call_target="tpu_custom_call" | custom-call | tf_op jit(solution)/shard_map/pallas_call | solution.py:411
  46.2 1.7 %shard_map.112 = (bf16[1,16,8,8,512]{4,3,2,1,0:T(8,128)(2,1)}, f32[16,16,64]{2,1,0:T(8,128)}, f32[16,16]{1,0:T(8,128)}, f32[1,16]{1,0:T(1,128)}) custom-call(f32[8,128,512]{2,1,0:T(8,128)S(1)} %get-tuple-element.14.acc, bf16[1,64,8,128]{3,2,1,0:T(8,128)(2,1)S(1)} %get-tuple-element.15.ad, f32[8,16,8,128]{3,2,1,0:T(8,128)S(1)} %get-tuple-element.16.su, ...), custom_call_target="tpu_custom_call" | custom-call | tf_op jit(solution)/shard_map/pallas_call | solution.py:468

commit v4 on v3

--- a/solution.py
+++ b/solution.py
@@ -151,13 +151,13 @@
 
     small[0].wait()
     for q in range(Q):
-        for r in range(0, R, 2):
+        for r in range(0, R, 4):
             x = q * R + r
-            f_copy(x).wait()
-            f_copy(x + 1).wait()
-            rows = jnp.concatenate([rows_of(f_v, x), rows_of(f_v, x + 1)], axis=0)
+            for t in range(4):
+                f_copy(x + t).wait()
+            rows = f_v[pl.ds(x, 4)].reshape(4 * CY, Z)
             depth = dot(tz[...], rows, 1, 1)
-            for t in range(2):
+            for t in range(4):
                 stage[q, pl.ds(r + t, S, stride=R), :] = depth[:, t * CY : (t + 1) * CY]
         su_s[q] = stage[q].astype(BF16).reshape(S, R, CY)
         if q == 0:
@@ -235,10 +235,10 @@
         for r in range(R):
             x = q * R + r
             g_v[x] = (rows_of(c_v, x).astype(F32) * gelu_slope(acc_v[x])).astype(BF16)
-        for r in range(0, R, 2):
+        for r in range(0, R, 4):
             x = q * R + r
-            depth = dot(tz[...], jnp.concatenate([g_v[x], g_v[x + 1]], axis=0), 1, 1)
-            for t in range(2):
+            depth = dot(tz[...], g_v[pl.ds(x, 4)].reshape(4 * CY, Z), 1, 1)
+            for t in range(4):
                 part = depth[:, t * CY : (t + 1) * CY]
                 stage[q, pl.ds(r + t, S, stride=R), :] = part
                 bias_sum = bias_sum + part[0:1, :]

time: 48 us -> 48 us (level)
  no operation moved by 1% of the time
where the time goes in v4:
time: 48 us; the launch traced here: 47.9 us
  Pallas kernels  47.2 us (98%)
  between operations  0.64 us (1%)
    pallas_call x1, Pallas kernels, shards(): pl.pallas_call(functools.partial(layer_kernel, sizes), out_shape=(shape((...  45.6 us
    pallas_call x1, Pallas kernels, shards(): pl.pallas_call(functools.partial(result_kernel, sizes), out_shape=(shape(...  1.65 us

profile of v4, /device:TPU:1, one launch (start us, length us, event | category | flops | bytes accessed | tf_op | source)
XLA Modules:
  0.0 47.9 jit_solution(2091346608759701066)
XLA Ops:
  0.6 45.6 %shard_map.111 = (f32[8,128,512]{2,1,0:T(8,128)S(1)}, bf16[1,64,8,128]{3,2,1,0:T(8,128)(2,1)S(1)}, f32[8,16,8,128]{3,2,1,0:T(8,128)S(1)}, bf16[8,8,8,128]{3,2,1,...) custom-call(bf16[1,16,8,8,512]{4,3,2,1,0:T(8,128)(2,1)} %fields.1, ...), custom_call_target="tpu_custom_call" | custom-call | tf_op jit(solution)/shard_map/pallas_call | solution.py:411
  46.2 1.7 %shard_map.112 = (bf16[1,16,8,8,512]{4,3,2,1,0:T(8,128)(2,1)}, f32[16,16,64]{2,1,0:T(8,128)}, f32[16,16]{1,0:T(8,128)}, f32[1,16]{1,0:T(1,128)}) custom-call(f32[8,128,512]{2,1,0:T(8,128)S(1)} %get-tuple-element.14.acc, bf16[1,64,8,128]{3,2,1,0:T(8,128)(2,1)S(1)} %get-tuple-element.15.ad, f32[8,16,8,128]{3,2,1,0:T(8,128)S(1)} %get-tuple-element.16.su, ...), custom_call_target="tpu_custom_call" | custom-call | tf_op jit(solution)/shard_map/pallas_call | solution.py:468
